TPU v7x, 32 devices: a whole 2x2x4 slice. The times are simulated.
32 devices in a mesh: cell: 16 (over z, y, x), gpt: 2 (over core).
Axes of the slice: x: 2, y: 2, z: 4, core: 2. Of those that a mesh axis runs over, the one named last changes fastest.
Arguments:
- fields: bfloat16 [6, 16, 131072], P(None, None, 'cell'), may hold values from 0.00099 to 0.1002, as said below
- surface: bfloat16 [2, 131072], P(None, 'cell'), may hold values from 0.19921875 to 0.94921875
- sunlit: int32 [131072], P('cell'), may hold values from 0 to 1
- routing: int32 [1024], P('cell'), may hold values from -1 to 15, as said below
- stencil: int32 [7, 131072], P(None, 'cell'), may hold values from -128 to 128
- weights: float32 [7, 131072], P(None, 'cell'), may hold values from 0.1 to 1
- optics: float32 [3, 112], P(None, 'gpt'), may hold values from 0.05 to 20
- solar_flux: float32 [112], P('gpt'), may hold values from 0.5 to 2
Outputs:
- heating_rate: float32 [16, 131072], P('gpt', 'cell')
Inputs may be any that keep to these rules, and one draw needn't show every extreme that they name: `routing`: each device is named by exactly 32 blocks in all, and by at most 4 of the 64 blocks of any one device. All fields are positive.
All inputs are finite; a program needn't handle non-finite values.
Results may differ from a plain program's by a relative error of at most 0.0003.
Values may be sent and summed in bfloat16 or wider, within the bound.
A program may use at most 64 MiB of HBM per device.

v0:
```python
import functools
import math

import jax
import jax.numpy as jnp
from jax import lax
from jax.experimental import pallas as pl
from jax.experimental.pallas import tpu as pltpu
from jax.sharding import PartitionSpec as P

G = 112
BLK = 128
HW = 128
ROWS = 8
WIDE = ROWS * BLK
LOG2E = math.log2(math.e)


def solve_kernel(
    levels,
    per_step,
    group_of,
    core_ref,
    routing_ref,
    optics_ref,
    flux_ref,
    fields_ref,
    surface_ref,
    sunlit_ref,
    keep_ref,
    send_ref,
    natural,
    packed,
    rows,
    total,
    turned,
):
    bands = flux_ref.shape[0]
    group = group_of(pl.program_id(0))
    core = core_ref[0]

    for b in range(ROWS):
        cols = pl.ds(b * BLK, BLK)
        here = pl.ds(b * levels, levels)
        cosine = surface_ref[0:1, cols].astype(jnp.float32)
        albedo = surface_ref[1:2, cols].astype(jnp.float32)
        scale = -LOG2E / cosine
        f = [fields_ref[k, :, cols].astype(jnp.float32) for k in range(6)]
        clouds = f[3] + f[4]
        natural[0, here, :] = scale * f[0]
        natural[1, here, :] = scale * f[1]
        natural[2, here, :] = scale * f[2]
        natural[3, here, :] = scale * (0.9 * clouds + 0.8 * f[5])
        natural[4, here, :] = scale * (0.1 * clouds + 0.2 * f[5])
        rows[0, b : b + 1, :] = scale
        rows[1, b : b + 1, :] = albedo * scale

    for level in range(levels):
        for k in range(5):
            packed[k, level] = natural[k, pl.ds(level, ROWS, stride=levels), :]
    scale = rows[0]
    for level in range(levels - 1):
        packed[5, level] = 0.5 * (packed[0, level] + packed[0, level + 1])
        packed[6, level] = 0.5 * (packed[3, level] + packed[3, level + 1]) + 0.1 * scale
    for level in range(levels):
        total[level] = jnp.zeros((ROWS, BLK), jnp.float32)

    def some_bands(step, carry):
        first = step * per_step
        lanes = range(per_step)
        kv = [optics_ref[0, first + i] for i in lanes]
        ko = [optics_ref[1, first + i] for i in lanes]
        kr = [optics_ref[2, first + i] for i in lanes]
        t = [LOG2E * jnp.log(jnp.full((ROWS, BLK), flux_ref[first + i], jnp.float32)) for i in lanes]
        half = 0.5 * rows[0]
        ratio = [None] * per_step
        rest = [None] * per_step
        filled = [None] * per_step
        kept = [[] for _ in lanes]
        for level in range(levels):
            last = level == levels - 1
            f0, f1, f2, cs, ca = [packed[k, level] for k in range(5)]
            if not last:
                f5, f6 = packed[5, level], packed[6, level]
            for i in lanes:
                s = kr[i] * f0 + cs
                a = kv[i] * f1 + (ko[i] * f2 + ca)
                t[i] = t[i] + (s + a)
                d = jnp.exp2(t[i])
                c = half if last else kr[i] * f5 + f6
                q = a + (half if level == 0 else ratio[i] * rest[i])
                inverse = pl.reciprocal(q + c, approx=True)
                z = ((s + rows[1]) if last else s) * d
                if level > 0:
                    z = z + ratio[i] * filled[i]
                rest[i], filled[i] = q, z
                ratio[i] = c * inverse
                kept[i].append((a, d, ratio[i], z * inverse))
        x = [None] * per_step
        for level in reversed(range(levels)):
            heat = total[level]
            for i in lanes:
                a, d, r, y = kept[i][level]
                x[i] = y if level == levels - 1 else y + r * x[i]
                heat = heat + a * (x[i] + d)
            total[level] = heat
        return carry

    lax.fori_loop(0, bands // per_step, some_bands, 0)

    for level in range(levels):
        turned[pl.ds(level, ROWS, stride=levels), :] = total[level]
    half_levels = levels // 2
    for b in range(ROWS):
        cols = pl.ds(b * BLK, BLK)
        cosine = surface_ref[0:1, cols].astype(jnp.float32)
        routed = (routing_ref[group * ROWS + b] >= 0).astype(jnp.float32)
        lit = sunlit_ref[b : b + 1, :].astype(jnp.float32) * routed
        weight = lit * (cosine * cosine) * (-1.0 / (LOG2E * G))
        mine = pl.multiple_of(b * levels + core * half_levels, half_levels)
        other = pl.multiple_of(b * levels + (1 - core) * half_levels, half_levels)
        keep_ref[:, cols] = turned[pl.ds(mine, half_levels), :] * weight
        send_ref[:, cols] = turned[pl.ds(other, half_levels), :] * weight


def solve_groups(core, routing, optics, flux, fields, surface, sunlit, group_of, count, per_step):
    levels = fields.shape[1]
    bands = flux.shape[0]
    half_levels = levels // 2
    smem = pl.BlockSpec(memory_space=pltpu.SMEM)
    out = pl.BlockSpec((half_levels, WIDE), lambda i: (0, i))
    shape = jax.ShapeDtypeStruct((half_levels, count * WIDE), jnp.float32)
    elements = count * WIDE * levels * bands
    return pl.pallas_call(
        functools.partial(solve_kernel, levels, per_step, group_of),
        grid=(count,),
        in_specs=[
            smem,
            smem,
            smem,
            smem,
            pl.BlockSpec((6, levels, WIDE), lambda i: (0, 0, group_of(i))),
            pl.BlockSpec((2, WIDE), lambda i: (0, group_of(i))),
            pl.BlockSpec((ROWS, BLK), lambda i: (group_of(i), 0)),
        ],
        out_specs=[out, out],
        out_shape=[shape, shape],
        scratch_shapes=[
            pltpu.VMEM((5, ROWS * levels, BLK), jnp.float32),
            pltpu.VMEM((7, levels, ROWS, BLK), jnp.float32),
            pltpu.VMEM((2, ROWS, BLK), jnp.float32),
            pltpu.VMEM((levels, ROWS, BLK), jnp.float32),
            pltpu.VMEM((ROWS * levels, BLK), jnp.float32),
        ],
        cost_estimate=pl.CostEstimate(
            flops=elements * 24, bytes_accessed=count * WIDE * levels * 20, transcendentals=elements * 2
        ),
    )(core, routing, optics, flux, fields, surface, sunlit)


def interpolate_kernel(
    edge_ref, edge_in_ref, mid_ref, mid_in_ref, low_ref, high_ref, stencil_ref, weights_ref, out_ref, wide
):
    columns = out_ref.shape[1]
    points = stencil_ref.shape[0]
    blocks = columns // BLK
    wide[:, 0:HW] = low_ref[...]
    wide[:, HW + columns : 2 * HW + columns] = high_ref[...]
    wide[:, HW : HW + WIDE] = edge_ref[:, 0:WIDE] + edge_in_ref[:, 0:WIDE]
    wide[:, HW + columns - WIDE : HW + columns] = edge_ref[:, WIDE:] + edge_in_ref[:, WIDE:]
    wide[:, HW + WIDE : HW + columns - WIDE] = mid_ref[...] + mid_in_ref[...]
    lane = lax.broadcasted_iota(jnp.int32, (points, BLK), 1) + HW

    def one_block(block, carry):
        start = pl.multiple_of(block * BLK, BLK)
        weights = weights_ref[:, pl.ds(start, BLK)]
        shares = weights / jnp.sum(weights, axis=0, keepdims=True)
        place = stencil_ref[:, pl.ds(start, BLK)] + lane
        which = place >> 7
        inner = place & (BLK - 1)
        sources = [wide[:, pl.ds(pl.multiple_of(start + k * BLK, BLK), BLK)] for k in range(3)]
        result = jnp.zeros(sources[0].shape, jnp.float32)
        for j in range(points):
            index = jnp.broadcast_to(inner[j : j + 1, :], result.shape)
            part = jnp.broadcast_to(which[j : j + 1, :], result.shape)
            got = [jnp.take_along_axis(s, index, axis=1, mode="promise_in_bounds") for s in sources]
            value = jnp.where(part == 0, got[0], jnp.where(part == 1, got[1], got[2]))
            result = result + shares[j : j + 1, :] * value
        out_ref[:, pl.ds(start, BLK)] = result
        return carry

    lax.fori_loop(0, blocks, one_block, 0, unroll=4)


def interpolate(edge, edge_in, mid, mid_in, low, high, stencil, weights):
    half_levels = low.shape[0]
    columns = stencil.shape[1]
    return pl.pallas_call(
        interpolate_kernel,
        in_specs=[pl.BlockSpec(memory_space=pltpu.VMEM)] * 8,
        out_specs=pl.BlockSpec(memory_space=pltpu.VMEM),
        out_shape=jax.ShapeDtypeStruct((half_levels, columns), jnp.float32),
        scratch_shapes=[pltpu.VMEM((half_levels, columns + 2 * HW), jnp.float32)],
        compiler_params=pltpu.CompilerParams(vmem_limit_bytes=16 * 1024 * 1024),
    )(edge, edge_in, mid, mid_in, low, high, stencil, weights)


def local(fields, surface, sunlit, routing, stencil, weights, optics, solar_flux):
    columns = fields.shape[2]
    groups = columns // WIDE
    count = lax.axis_size("cell")
    core = lax.axis_index("gpt").reshape(1)
    lit = sunlit.reshape(columns // BLK, BLK)
    solve = functools.partial(solve_groups, core, routing, optics, solar_flux, fields, surface, lit)
    swap = [(0, 1), (1, 0)]
    up = [(i, (i + 1) % count) for i in range(count)]
    down = [(b, a) for a, b in up]
    edge, edge_out = solve(lambda i: i * (groups - 1), 2, 2)
    edge_in = lax.ppermute(edge_out, "gpt", swap)
    mid, mid_out = solve(lambda i: i + 1, groups - 2, 2)
    low = lax.ppermute(edge[:, -HW:] + edge_in[:, -HW:], "cell", up)
    high = lax.ppermute(edge[:, :HW] + edge_in[:, :HW], "cell", down)
    mid_in = lax.ppermute(mid_out, "gpt", swap)
    return interpolate(edge, edge_in, mid, mid_in, low, high, stencil, weights)


def solution(mesh):
    placed = (
        P(None, None, "cell"),
        P(None, "cell"),
        P("cell"),
        P("cell"),
        P(None, "cell"),
        P(None, "cell"),
        P(None, "gpt"),
        P("gpt"),
    )
    return jax.shard_map(
        local, mesh=mesh, in_specs=placed, out_specs=P("gpt", "cell"), check_vma=False
    )
```

profile of v0, /device:TPU:0, one launch (start us, length us, event | category | flops | bytes accessed | tf_op | source)
XLA Modules:
  0.0 71.2 jit_solution(5093858876800441274)
XLA Ops:
  0.0 13.5 %shard_map.82 = (f32[8,2048]{1,0:T(8,128)}, f32[8,2048]{1,0:T(8,128)}) custom-call(s32[1]{0:T(128)} %bitcast.core_ref, s32[64]{0:T(128)} %routing_ref.3, f32[3,56]{1,0:T(4,128)} %optics_ref.3, f32[56]{0:T(128)} %flux_ref.3, bf16[6,16,8192]{2,1,0:T(8,128)(2,1)} %fields_ref.3, bf16[2,8192]{1,0:T(2,128)(2,1)} %surface_ref.3, s32[64,128]{1,0:T(8,128)} %bitcast.2), custom_call_target="tpu_custom_call" | custom-call | flops 44040192 | bytes 655360 | tf_op jit(solution)/shard_map/pallas_call | solution.py:134
  13.5 0.0 copy-start.3
  13.5 0.0 copy-start
  13.5 0.0 copy-start.1
  13.5 0.5 collective-permute-start
  14.0 37.3 %shard_map.83 = (f32[8,6144]{1,0:T(8,128)}, f32[8,6144]{1,0:T(8,128)}) custom-call(s32[1]{0:T(128)} %bitcast.core_ref, s32[64]{0:T(128)} %routing_ref.3, f32[3,56]{1,0:T(4,128)} %optics_ref.3, f32[56]{0:T(128)} %flux_ref.3, bf16[6,16,8192]{2,1,0:T(8,128)(2,1)} %fields_ref.3, bf16[2,8192]{1,0:T(2,128)(2,1)} %surface_ref.3, s32[64,128]{1,0:T(8,128)} %bitcast.3), custom_call_target="tpu_custom_call" | custom-call | flops 132120576 | bytes 1966080 | tf_op jit(solution)/shard_map/pallas_call | solution.py:134
  51.3 0.1 collective-permute-start.1
  51.4 0.0 collective-permute-done.edge_in_ref
  51.4 0.0 copy-done.3
  51.4 6.9 %collective-permute-start.3 = (f32[8,128]{1,0:T(8,128)S(1)}, f32[8,128]{1,0:T(8,128)S(1)}, u32[]{:S(2)}, u32[]{:S(2)}) collective-permute-start(f32[8,128]{1,0:T(8,128)S(1)} %get-tuple-element.13), channel_id=1, source_target_pairs={{2,0},{4,2},{6,4},{8,6},{10,8},{12,10},{14,12},{16,14},{18,16},{20... | collective-permute-start | bytes 12296 | tf_op jit(solution)/shard_map/ppermute | solution.py:222
  58.3 0.0 collective-permute-start.2
  58.3 1.3 %collective-permute-done.3.high_ref = f32[8,128]{1,0:T(8,128)S(1)} collective-permute-done((f32[8,128]{1,0:T(8,128)S(1)}, f32[8,128]{1,0:T(8,128)S(1)}, u32[]{:S(2)}, u32[]{:S(2)}) %collective-permute-start.3) | collective-permute-done | bytes 4128 | tf_op jit(solution)/shard_map/ppermute | solution.py:222
  59.7 5.9 %collective-permute-done.2.low_ref = f32[8,128]{1,0:T(8,128)S(1)} collective-permute-done((f32[8,128]{1,0:T(8,128)S(1)}, f32[8,128]{1,0:T(8,128)S(1)}, u32[]{:S(2)}, u32[]{:S(2)}) %collective-permute-start.2) | collective-permute-done | bytes 4128 | tf_op jit(solution)/shard_map/ppermute | solution.py:221
  65.5 0.0 collective-permute-done.1.mid_in_ref
  65.5 0.0 copy-done
  65.5 0.0 copy-done.1
  65.6 0.0 copy-start.2
  65.6 0.9 %copy-done.2 = f32[8,6144]{1,0:T(8,128)S(1)} copy-done((f32[8,6144]{1,0:T(8,128)S(1)}, f32[8,6144]{1,0:T(8,128)}, u32[]{:S(2)}) %copy-start.2) | copy-done | bytes 196632
  66.5 4.7 %shard_map.84 = f32[8,8192]{1,0:T(8,128)} custom-call(f32[8,2048]{1,0:T(8,128)S(1)} %copy-done.3, f32[8,2048]{1,0:T(8,128)S(1)} %collective-permute-done.edge_in_ref, f32[8,6144]{1,0:T(8,128)S(1)} %copy-done.2, f32[8,6144]{1,0:T(8,128)S(1)} %collective-permute-done.1.mid_in_ref, f32[8,128]{1,0:T(8,128)S(1)} %collective-permute-done.2.low_ref, ...), custom_call_target="tpu_custom_call" | custom-call | tf_op jit(solution)/shard_map/pallas_call | solution.py:198
  (1 shorter events, 0.0 us)
Async XLA Ops:
  13.5 37.9 %copy-start.3 = (f32[8,2048]{1,0:T(8,128)S(1)}, f32[8,2048]{1,0:T(8,128)}, u32[]{:S(2)}) copy-start(f32[8,2048]{1,0:T(8,128)} %get-tuple-element.9.edge_ref) | copy-start | bytes 196612
  13.5 52.1 %copy-start = (s32[7,8192]{1,0:T(8,128)S(1)}, s32[7,8192]{1,0:T(8,128)}, u32[]{:S(2)}) copy-start(s32[7,8192]{1,0:T(8,128)} %stencil_ref.1) | copy-start | bytes 688132
  13.5 52.1 %copy-start.1 = (f32[7,8192]{1,0:T(8,128)S(1)}, f32[7,8192]{1,0:T(8,128)}, u32[]{:S(2)}) copy-start(f32[7,8192]{1,0:T(8,128)} %weights_ref.1) | copy-start | bytes 688132
  13.5 37.9 %collective-permute-start = (f32[8,2048]{1,0:T(8,128)}, f32[8,2048]{1,0:T(8,128)S(1)}, u32[]{:S(2)}, u32[]{:S(2)}) collective-permute-start(f32[8,2048]{1,0:T(8,128)} %get-tuple-element.10), channel_id=1, source_target_pairs={{0,1},{1,0},{2,3},{3,2},{4,5},{5,4},{6,7},{7,6},{8,9},{9,8},{10,11... | collective-permute-start | bytes 196616 | tf_op jit(solution)/shard_map/ppermute | solution.py:219
  51.3 14.3 %collective-permute-start.1 = (f32[8,6144]{1,0:T(8,128)}, f32[8,6144]{1,0:T(8,128)S(1)}, u32[]{:S(2)}, u32[]{:S(2)}) collective-permute-start(f32[8,6144]{1,0:T(8,128)} %get-tuple-element.12), channel_id=1, source_target_pairs={{0,1},{1,0},{2,3},{3,2},{4,5},{5,4},{6,7},{7,6},{8,9},{9,8},{10,11... | collective-permute-start | bytes 589832 | tf_op jit(solution)/shard_map/ppermute | solution.py:223
  51.4 8.3 %collective-permute-start.3 = (f32[8,128]{1,0:T(8,128)S(1)}, f32[8,128]{1,0:T(8,128)S(1)}, u32[]{:S(2)}, u32[]{:S(2)}) collective-permute-start(f32[8,128]{1,0:T(8,128)S(1)} %get-tuple-element.13), channel_id=1, source_target_pairs={{2,0},{4,2},{6,4},{8,6},{10,8},{12,10},{14,12},{16,14},{18,16},{20... | collective-permute-start | bytes 12296 | tf_op jit(solution)/shard_map/ppermute | solution.py:222
  58.3 7.2 %collective-permute-start.2 = (f32[8,128]{1,0:T(8,128)S(1)}, f32[8,128]{1,0:T(8,128)S(1)}, u32[]{:S(2)}, u32[]{:S(2)}) collective-permute-start(f32[8,128]{1,0:T(8,128)S(1)} %get-tuple-element.14), channel_id=1, source_target_pairs={{0,2},{2,4},{4,6},{6,8},{8,10},{10,12},{12,14},{14,16},{16,18},{18... | collective-permute-start | bytes 12296 | tf_op jit(solution)/shard_map/ppermute | solution.py:221
  65.6 0.9 %copy-start.2 = (f32[8,6144]{1,0:T(8,128)S(1)}, f32[8,6144]{1,0:T(8,128)}, u32[]{:S(2)}) copy-start(f32[8,6144]{1,0:T(8,128)} %get-tuple-element.11.mid_ref) | copy-start | bytes 589828
where the time goes:
time: 71.4 us; the launch traced here: 71.2 us
  Pallas kernels  55.4 us (78%)
  starting transfers between devices  7.58 us (11%)
  waiting for transfers between devices  7.2 us (10%)
  local copies, waits for them, and re-layouts  0.94 us (1%)
    pallas_call x2, Pallas kernels, solve_groups(): pl.pallas_call(functools.partial(solve_kernel, levels, per_step, group_of...  50.7 us
    ppermute x1, starting transfers between devices, local(): high = lax.ppermute(edge[:, :HW] + edge_in[:, :HW], 'cell', down)  6.94 us
    ppermute x1, waiting for transfers between devices, local(): low = lax.ppermute(edge[:, -HW:] + edge_in[:, -HW:], 'cell', up)  5.87 us
    pallas_call x1, Pallas kernels, interpolate(): pl.pallas_call(interpolate_kernel, in_specs=[pl.BlockSpec(memory_space=pl...  4.71 us
  transfers between devices with their start and end apart: 4, of which 2 were waited for; matrix products, arithmetic and copies ran while one was open for 0% of the time, Pallas kernels for 52%

commit v1 on v0

--- a/solution.py
+++ b/solution.py
@@ -34,6 +34,8 @@
     rows,
     total,
     turned,
+    slot_a,
+    slot_b,
 ):
     bands = flux_ref.shape[0]
     group = group_of(pl.program_id(0))
@@ -65,7 +67,7 @@
     for level in range(levels):
         total[level] = jnp.zeros((ROWS, BLK), jnp.float32)
 
-    def some_bands(step, carry):
+    def ahead(step, slot):
         first = step * per_step
         lanes = range(per_step)
         kv = [optics_ref[0, first + i] for i in lanes]
@@ -76,7 +78,6 @@
         ratio = [None] * per_step
         rest = [None] * per_step
         filled = [None] * per_step
-        kept = [[] for _ in lanes]
         for level in range(levels):
             last = level == levels - 1
             f0, f1, f2, cs, ca = [packed[k, level] for k in range(5)]
@@ -95,18 +96,42 @@
                     z = z + ratio[i] * filled[i]
                 rest[i], filled[i] = q, z
                 ratio[i] = c * inverse
-                kept[i].append((a, d, ratio[i], z * inverse))
+                slot[0, level, i] = a
+                slot[1, level, i] = d
+                slot[2, level, i] = z * inverse
+                if not last:
+                    slot[3, level, i] = ratio[i]
+            yield
+
+    def back(slot):
         x = [None] * per_step
         for level in reversed(range(levels)):
             heat = total[level]
-            for i in lanes:
-                a, d, r, y = kept[i][level]
-                x[i] = y if level == levels - 1 else y + r * x[i]
-                heat = heat + a * (x[i] + d)
+            for i in range(per_step):
+                y = slot[2, level, i]
+                x[i] = y if level == levels - 1 else y + slot[3, level, i] * x[i]
+                heat = heat + slot[0, level, i] * (x[i] + slot[1, level, i])
             total[level] = heat
+            yield
+
+    def run(*parts):
+        for _ in zip(*parts):
+            pass
+
+    steps = bands // per_step
+    run(ahead(0, slot_a))
+
+    def two_steps(k, carry):
+        run(ahead(2 * k + 1, slot_b), back(slot_a))
+        run(ahead(2 * k + 2, slot_a), back(slot_b))
         return carry
 
-    lax.fori_loop(0, bands // per_step, some_bands, 0)
+    lax.fori_loop(0, (steps - 1) // 2, two_steps, 0)
+    if steps % 2:
+        run(back(slot_a))
+    else:
+        run(ahead(steps - 1, slot_b), back(slot_a))
+        run(back(slot_b))
 
     for level in range(levels):
         turned[pl.ds(level, ROWS, stride=levels), :] = total[level]
@@ -151,6 +176,8 @@
             pltpu.VMEM((2, ROWS, BLK), jnp.float32),
             pltpu.VMEM((levels, ROWS, BLK), jnp.float32),
             pltpu.VMEM((ROWS * levels, BLK), jnp.float32),
+            pltpu.VMEM((4, levels, per_step, ROWS, BLK), jnp.float32),
+            pltpu.VMEM((4, levels, per_step, ROWS, BLK), jnp.float32),
         ],
         cost_estimate=pl.CostEstimate(
             flops=elements * 24, bytes_accessed=count * WIDE * levels * 20, transcendentals=elements * 2
@@ -158,17 +185,65 @@
     )(core, routing, optics, flux, fields, surface, sunlit)
 
 
-def interpolate_kernel(
-    edge_ref, edge_in_ref, mid_ref, mid_in_ref, low_ref, high_ref, stencil_ref, weights_ref, out_ref, wide
-):
+def exchange_kernel(keep_ref, send_ref, near_ref, halo_ref, send_sem, recv_sem):
+    count = lax.axis_size("cell")
+    cell = lax.axis_index("cell")
+    core = lax.axis_index("gpt")
+    columns = keep_ref.shape[1]
+    after, before = lax.rem(cell + 1, count), lax.rem(cell + count - 1, count)
+    partners = [(cell, 1 - core), (after, core), (after, 1 - core), (before, core), (before, 1 - core)]
+    barrier = pltpu.get_barrier_semaphore()
+    for partner in partners:
+        pl.semaphore_signal(barrier, inc=1, device_id=partner, device_id_type=pl.DeviceIdType.MESH)
+    pl.semaphore_wait(barrier, len(partners))
+    tail = pl.ds(columns - HW, HW)
+    head = pl.ds(0, HW)
+    copies = [
+        (keep_ref.at[:, tail], halo_ref.at[0]),
+        (send_ref.at[:, tail], halo_ref.at[1]),
+        (keep_ref.at[:, head], halo_ref.at[2]),
+        (send_ref.at[:, head], halo_ref.at[3]),
+        (send_ref, near_ref),
+    ]
+    started = []
+    for k, (source, target) in enumerate(copies):
+        copy = pltpu.make_async_remote_copy(
+            src_ref=source,
+            dst_ref=target,
+            send_sem=send_sem.at[k],
+            recv_sem=recv_sem.at[k],
+            device_id=(partners[1:] + partners[:1])[k],
+            device_id_type=pl.DeviceIdType.MESH,
+        )
+        copy.start()
+        started.append(copy)
+    for copy in started:
+        copy.wait()
+
+
+def exchange(keep, send):
+    half_levels = keep.shape[0]
+    vmem = pl.BlockSpec(memory_space=pltpu.VMEM)
+    return pl.pallas_call(
+        exchange_kernel,
+        in_specs=[vmem] * 2,
+        out_specs=[vmem] * 2,
+        out_shape=[
+            jax.ShapeDtypeStruct(send.shape, jnp.float32),
+            jax.ShapeDtypeStruct((4, half_levels, HW), jnp.float32),
+        ],
+        scratch_shapes=[pltpu.SemaphoreType.DMA((5,)), pltpu.SemaphoreType.DMA((5,))],
+        compiler_params=pltpu.CompilerParams(collective_id=0, has_side_effects=True),
+    )(keep, send)
+
+
+def interpolate_kernel(keep_ref, near_ref, halo_ref, stencil_ref, weights_ref, out_ref, wide):
     columns = out_ref.shape[1]
     points = stencil_ref.shape[0]
     blocks = columns // BLK
-    wide[:, 0:HW] = low_ref[...]
-    wide[:, HW + columns : 2 * HW + columns] = high_ref[...]
-    wide[:, HW : HW + WIDE] = edge_ref[:, 0:WIDE] + edge_in_ref[:, 0:WIDE]
-    wide[:, HW + columns - WIDE : HW + columns] = edge_ref[:, WIDE:] + edge_in_ref[:, WIDE:]
-    wide[:, HW + WIDE : HW + columns - WIDE] = mid_ref[...] + mid_in_ref[...]
+    wide[:, 0:HW] = halo_ref[0] + halo_ref[1]
+    wide[:, HW + columns : 2 * HW + columns] = halo_ref[2] + halo_ref[3]
+    wide[:, HW : HW + columns] = keep_ref[...] + near_ref[...]
     lane = lax.broadcasted_iota(jnp.int32, (points, BLK), 1) + HW
 
     def one_block(block, carry):
@@ -192,36 +267,28 @@
     lax.fori_loop(0, blocks, one_block, 0, unroll=4)
 
 
-def interpolate(edge, edge_in, mid, mid_in, low, high, stencil, weights):
-    half_levels = low.shape[0]
-    columns = stencil.shape[1]
+def interpolate(*operands):
+    half_levels = operands[0].shape[0]
+    columns = operands[-1].shape[1]
     return pl.pallas_call(
         interpolate_kernel,
-        in_specs=[pl.BlockSpec(memory_space=pltpu.VMEM)] * 8,
+        in_specs=[pl.BlockSpec(memory_space=pltpu.VMEM)] * len(operands),
         out_specs=pl.BlockSpec(memory_space=pltpu.VMEM),
         out_shape=jax.ShapeDtypeStruct((half_levels, columns), jnp.float32),
         scratch_shapes=[pltpu.VMEM((half_levels, columns + 2 * HW), jnp.float32)],
         compiler_params=pltpu.CompilerParams(vmem_limit_bytes=16 * 1024 * 1024),
-    )(edge, edge_in, mid, mid_in, low, high, stencil, weights)
+    )(*operands)
 
 
 def local(fields, surface, sunlit, routing, stencil, weights, optics, solar_flux):
     columns = fields.shape[2]
     groups = columns // WIDE
-    count = lax.axis_size("cell")
     core = lax.axis_index("gpt").reshape(1)
     lit = sunlit.reshape(columns // BLK, BLK)
     solve = functools.partial(solve_groups, core, routing, optics, solar_flux, fields, surface, lit)
-    swap = [(0, 1), (1, 0)]
-    up = [(i, (i + 1) % count) for i in range(count)]
-    down = [(b, a) for a, b in up]
-    edge, edge_out = solve(lambda i: i * (groups - 1), 2, 2)
-    edge_in = lax.ppermute(edge_out, "gpt", swap)
-    mid, mid_out = solve(lambda i: i + 1, groups - 2, 2)
-    low = lax.ppermute(edge[:, -HW:] + edge_in[:, -HW:], "cell", up)
-    high = lax.ppermute(edge[:, :HW] + edge_in[:, :HW], "cell", down)
-    mid_in = lax.ppermute(mid_out, "gpt", swap)
-    return interpolate(edge, edge_in, mid, mid_in, low, high, stencil, weights)
+    keep, send = solve(lambda i: i, groups, 4)
+    near, halo = exchange(keep, send)
+    return interpolate(keep, near, halo, stencil, weights)
 
 
 def solution(mesh):

time: 71.4 us -> 47 us (0.66)
  Pallas kernels: 55.4 us -> 44.1 us
  starting transfers between devices: 7.58 us -> 0 us
  waiting for transfers between devices: 7.2 us -> 0 us
  local copies, waits for them, and re-layouts: 0.94 us -> 2.62 us
    pallas_call x2 -> x1, Pallas kernels: 50.7 us -> 28.5 us  [solve_groups(): pl.pallas_call(functools.partial(solve_kernel, levels, per_step, group_of...]
    pallas_call x0 -> x1, Pallas kernels: none -> 10.9 us  [exchange(): pl.pallas_call(exchange_kernel, in_specs=[vmem] * 2, out_specs=[vmem] * 2...]
    ppermute x4 -> x0, starting transfers between devices: 7.58 us -> none  [the longest x1 6.94 us: local(): high = lax.ppermute(edge[:, :HW] + edge_in[:, :HW], 'cell', down)]
    ppermute x4 -> x0, waiting for transfers between devices: 7.2 us -> none  [the longest x1 5.87 us: local(): low = lax.ppermute(edge[:, -HW:] + edge_in[:, -HW:], 'cell', up)]
    unnamed x8 -> x10, local copies, waits for them, and re-layouts: 0.94 us -> 2.62 us
  transfers between devices with their start and end apart: 4 -> 0, of which waited for: 2 -> 0; matrix products, arithmetic and copies ran while one was open for 0% -> 0% of each run, Pallas kernels for 52% -> 0%
where the time goes in v1:
time: 47 us; the launch traced here: 46.7 us
  Pallas kernels  44.1 us (94%)
  local copies, waits for them, and re-layouts  2.62 us (6%)
    pallas_call x1, Pallas kernels, solve_groups(): pl.pallas_call(functools.partial(solve_kernel, levels, per_step, group_of...  28.5 us
    pallas_call x1, Pallas kernels, exchange(): pl.pallas_call(exchange_kernel, in_specs=[vmem] * 2, out_specs=[vmem] * 2...  10.9 us
    pallas_call x1, Pallas kernels, interpolate(): pl.pallas_call(interpolate_kernel, in_specs=[pl.BlockSpec(memory_space=pl...  4.71 us
    unnamed x10, local copies, waits for them, and re-layouts  2.62 us

profile of v1, /device:TPU:0, one launch (start us, length us, event | category | flops | bytes accessed | tf_op | source)
XLA Modules:
  0.0 46.7 jit_solution(3753821936261220922)
XLA Ops:
  0.0 0.0 copy-start.1
  0.0 0.0 copy-start.2
  0.0 28.5 %shard_map.82 = (f32[8,8192]{1,0:T(8,128)}, f32[8,8192]{1,0:T(8,128)}) custom-call(s32[1]{0:T(128)} %bitcast.core_ref, s32[64]{0:T(128)} %routing_ref.1, f32[3,56]{1,0:T(4,128)} %optics_ref.1, f32[56]{0:T(128)} %flux_ref.1, bf16[6,16,8192]{2,1,0:T(8,128)(2,1)} %fields_ref.1, bf16[2,8192]{1,0:T(2,128)(2,1)} %surface_ref.1, s32[64,128]{1,0:T(8,128)} %bitcast.2), custom_call_target="tpu_custom_call" | custom-call | flops 176160768 | bytes 2621440 | tf_op jit(solution)/shard_map/pallas_call | solution.py:159
  28.5 10.9 %shard_map.83 = (f32[8,8192]{1,0:T(8,128)}, f32[4,8,128]{2,1,0:T(8,128)}) custom-call(f32[8,8192]{1,0:T(8,128)} %get-tuple-element.9.keep_ref, f32[8,8192]{1,0:T(8,128)} %get-tuple-element.10.send_ref), custom_call_target="tpu_custom_call" | custom-call | tf_op jit(solution)/shard_map/pallas_call | solution.py:227
  39.4 0.0 copy-done.1
  39.4 0.0 copy-done.2
  39.4 0.0 copy-start
  39.4 0.9 %copy-done = f32[8,8192]{1,0:T(8,128)S(1)} copy-done((f32[8,8192]{1,0:T(8,128)S(1)}, f32[8,8192]{1,0:T(8,128)}, u32[]{:S(2)}) %copy-start) | copy-done | bytes 262168
  40.4 0.0 copy-start.3
  40.4 0.9 %copy-done.3 = f32[8,8192]{1,0:T(8,128)S(1)} copy-done((f32[8,8192]{1,0:T(8,128)S(1)}, f32[8,8192]{1,0:T(8,128)}, u32[]{:S(2)}) %copy-start.3) | copy-done | bytes 262168
  41.3 0.0 copy-start.4
  41.3 0.7 %copy-done.4 = f32[4,8,128]{2,1,0:T(8,128)S(1)} copy-done((f32[4,8,128]{2,1,0:T(8,128)S(1)}, f32[4,8,128]{2,1,0:T(8,128)}, u32[]{:S(2)}) %copy-start.4) | copy-done | bytes 16408
  42.0 4.7 %shard_map.84 = f32[8,8192]{1,0:T(8,128)} custom-call(f32[8,8192]{1,0:T(8,128)S(1)} %copy-done, f32[8,8192]{1,0:T(8,128)S(1)} %copy-done.3, f32[4,8,128]{2,1,0:T(8,128)S(1)} %copy-done.4, s32[7,8192]{1,0:T(8,128)S(1)} %copy-done.1, f32[7,8192]{1,0:T(8,128)S(1)} %copy-done.2), custom_call_target="tpu_custom_call" | custom-call | tf_op jit(solution)/shard_map/pallas_call | solution.py:273
Async XLA Ops:
  0.0 39.4 %copy-start.1 = (s32[7,8192]{1,0:T(8,128)S(1)}, s32[7,8192]{1,0:T(8,128)}, u32[]{:S(2)}) copy-start(s32[7,8192]{1,0:T(8,128)} %stencil_ref.1) | copy-start | bytes 688132
  0.0 39.4 %copy-start.2 = (f32[7,8192]{1,0:T(8,128)S(1)}, f32[7,8192]{1,0:T(8,128)}, u32[]{:S(2)}) copy-start(f32[7,8192]{1,0:T(8,128)} %weights_ref.1) | copy-start | bytes 688132
  39.4 1.0 %copy-start = (f32[8,8192]{1,0:T(8,128)S(1)}, f32[8,8192]{1,0:T(8,128)}, u32[]{:S(2)}) copy-start(f32[8,8192]{1,0:T(8,128)} %get-tuple-element.9.keep_ref) | copy-start | bytes 786436
  40.4 0.9 %copy-start.3 = (f32[8,8192]{1,0:T(8,128)S(1)}, f32[8,8192]{1,0:T(8,128)}, u32[]{:S(2)}) copy-start(f32[8,8192]{1,0:T(8,128)} %get-tuple-element.11.near_ref) | copy-start | bytes 786436
  41.3 0.7 %copy-start.4 = (f32[4,8,128]{2,1,0:T(8,128)S(1)}, f32[4,8,128]{2,1,0:T(8,128)}, u32[]{:S(2)}) copy-start(f32[4,8,128]{2,1,0:T(8,128)} %get-tuple-element.12.halo_ref) | copy-start | bytes 49156

commit v2 on v1

--- a/solution.py
+++ b/solution.py
@@ -185,13 +185,16 @@
     )(core, routing, optics, flux, fields, surface, sunlit)
 
 
-def exchange_kernel(keep_ref, send_ref, near_ref, halo_ref, send_sem, recv_sem):
+def exchange_kernel(keep_ref, send_ref, wide_ref, near_ref, halo_ref, own_sem, send_sem, recv_sem):
     count = lax.axis_size("cell")
     cell = lax.axis_index("cell")
     core = lax.axis_index("gpt")
     columns = keep_ref.shape[1]
     after, before = lax.rem(cell + 1, count), lax.rem(cell + count - 1, count)
     partners = [(cell, 1 - core), (after, core), (after, 1 - core), (before, core), (before, 1 - core)]
+    middle = pl.ds(HW, columns)
+    own = pltpu.make_async_copy(keep_ref, wide_ref.at[:, middle], own_sem)
+    own.start()
     barrier = pltpu.get_barrier_semaphore()
     for partner in partners:
         pl.semaphore_signal(barrier, inc=1, device_id=partner, device_id_type=pl.DeviceIdType.MESH)
@@ -217,33 +220,37 @@
         )
         copy.start()
         started.append(copy)
+    own.wait()
     for copy in started:
         copy.wait()
+    wide_ref[:, 0:HW] = halo_ref[0] + halo_ref[1]
+    wide_ref[:, HW + columns : 2 * HW + columns] = halo_ref[2] + halo_ref[3]
+    wide_ref[:, middle] = wide_ref[:, middle] + near_ref[...]
 
 
 def exchange(keep, send):
-    half_levels = keep.shape[0]
-    vmem = pl.BlockSpec(memory_space=pltpu.VMEM)
+    half_levels, columns = keep.shape
     return pl.pallas_call(
         exchange_kernel,
-        in_specs=[vmem] * 2,
-        out_specs=[vmem] * 2,
-        out_shape=[
-            jax.ShapeDtypeStruct(send.shape, jnp.float32),
-            jax.ShapeDtypeStruct((4, half_levels, HW), jnp.float32),
+        in_specs=[pl.BlockSpec(memory_space=pl.ANY)] * 2,
+        out_specs=pl.BlockSpec(memory_space=pltpu.VMEM),
+        out_shape=jax.ShapeDtypeStruct((half_levels, columns + 2 * HW), jnp.float32),
+        scratch_shapes=[
+            pltpu.VMEM((half_levels, columns), jnp.float32),
+            pltpu.VMEM((4, half_levels, HW), jnp.float32),
+            pltpu.SemaphoreType.DMA,
+            pltpu.SemaphoreType.DMA((5,)),
+            pltpu.SemaphoreType.DMA((5,)),
         ],
-        scratch_shapes=[pltpu.SemaphoreType.DMA((5,)), pltpu.SemaphoreType.DMA((5,))],
         compiler_params=pltpu.CompilerParams(collective_id=0, has_side_effects=True),
     )(keep, send)
 
 
-def interpolate_kernel(keep_ref, near_ref, halo_ref, stencil_ref, weights_ref, out_ref, wide):
+def interpolate_kernel(wide, stencil_ref, weights_ref, out_ref):
     columns = out_ref.shape[1]
     points = stencil_ref.shape[0]
     blocks = columns // BLK
-    wide[:, 0:HW] = halo_ref[0] + halo_ref[1]
-    wide[:, HW + columns : 2 * HW + columns] = halo_ref[2] + halo_ref[3]
-    wide[:, HW : HW + columns] = keep_ref[...] + near_ref[...]
+    base = pl.program_id(0) * columns
     lane = lax.broadcasted_iota(jnp.int32, (points, BLK), 1) + HW
 
     def one_block(block, carry):
@@ -253,7 +260,7 @@
         place = stencil_ref[:, pl.ds(start, BLK)] + lane
         which = place >> 7
         inner = place & (BLK - 1)
-        sources = [wide[:, pl.ds(pl.multiple_of(start + k * BLK, BLK), BLK)] for k in range(3)]
+        sources = [wide[:, pl.ds(pl.multiple_of(base + start + k * BLK, BLK), BLK)] for k in range(3)]
         result = jnp.zeros(sources[0].shape, jnp.float32)
         for j in range(points):
             index = jnp.broadcast_to(inner[j : j + 1, :], result.shape)
@@ -264,20 +271,21 @@
         out_ref[:, pl.ds(start, BLK)] = result
         return carry
 
-    lax.fori_loop(0, blocks, one_block, 0, unroll=4)
-
-
-def interpolate(*operands):
-    half_levels = operands[0].shape[0]
-    columns = operands[-1].shape[1]
+    lax.fori_loop(0, blocks, one_block, 0, unroll=8)
+
+
+def interpolate(wide, stencil, weights):
+    half_levels = wide.shape[0]
+    points, columns = stencil.shape
+    part = 4 * WIDE
+    piece = pl.BlockSpec((points, part), lambda i: (0, i))
     return pl.pallas_call(
         interpolate_kernel,
-        in_specs=[pl.BlockSpec(memory_space=pltpu.VMEM)] * len(operands),
-        out_specs=pl.BlockSpec(memory_space=pltpu.VMEM),
+        grid=(columns // part,),
+        in_specs=[pl.BlockSpec(memory_space=pltpu.VMEM), piece, piece],
+        out_specs=pl.BlockSpec((half_levels, part), lambda i: (0, i)),
         out_shape=jax.ShapeDtypeStruct((half_levels, columns), jnp.float32),
-        scratch_shapes=[pltpu.VMEM((half_levels, columns + 2 * HW), jnp.float32)],
-        compiler_params=pltpu.CompilerParams(vmem_limit_bytes=16 * 1024 * 1024),
-    )(*operands)
+    )(wide, stencil, weights)
 
 
 def local(fields, surface, sunlit, routing, stencil, weights, optics, solar_flux):
@@ -287,8 +295,7 @@
     lit = sunlit.reshape(columns // BLK, BLK)
     solve = functools.partial(solve_groups, core, routing, optics, solar_flux, fields, surface, lit)
     keep, send = solve(lambda i: i, groups, 4)
-    near, halo = exchange(keep, send)
-    return interpolate(keep, near, halo, stencil, weights)
+    return interpolate(exchange(keep, send), stencil, weights)
 
 
 def solution(mesh):

time: 47 us -> 43.9 us (0.934)
  local copies, waits for them, and re-layouts: 2.62 us -> 0 us
    unnamed x10 -> x0, local copies, waits for them, and re-layouts: 2.62 us -> none
where the time goes in v2:
time: 43.9 us; the launch traced here: 43.7 us
  Pallas kernels  43.7 us (100%)
    pallas_call x1, Pallas kernels, solve_groups(): pl.pallas_call(functools.partial(solve_kernel, levels, per_step, group_of...  28.4 us
    pallas_call x1, Pallas kernels, exchange(): pl.pallas_call(exchange_kernel, in_specs=[pl.BlockSpec(memory_space=pl.AN...  10.1 us
    pallas_call x1, Pallas kernels, interpolate(): pl.pallas_call(interpolate_kernel, grid=(columns // part,), in_specs=[pl....  5.19 us

profile of v2, /device:TPU:0, one launch (start us, length us, event | category | flops | bytes accessed | tf_op | source)
XLA Modules:
  0.0 43.7 jit_solution(8752515837611893056)
XLA Ops:
  0.0 28.4 %shard_map.82 = (f32[8,8192]{1,0:T(8,128)}, f32[8,8192]{1,0:T(8,128)}) custom-call(s32[1]{0:T(128)} %bitcast.core_ref, s32[64]{0:T(128)} %routing_ref.1, f32[3,56]{1,0:T(4,128)} %optics_ref.1, f32[56]{0:T(128)} %flux_ref.1, bf16[6,16,8192]{2,1,0:T(8,128)(2,1)} %fields_ref.1, bf16[2,8192]{1,0:T(2,128)(2,1)} %surface_ref.1, s32[64,128]{1,0:T(8,128)} %bitcast.2), custom_call_target="tpu_custom_call" | custom-call | flops 176160768 | bytes 2621440 | tf_op jit(solution)/shard_map/pallas_call | solution.py:159
  28.4 10.1 %shard_map.83.wide = f32[8,8448]{1,0:T(8,128)} custom-call(f32[8,8192]{1,0:T(8,128)} %get-tuple-element.7.keep_ref, f32[8,8192]{1,0:T(8,128)} %get-tuple-element.8.send_ref), custom_call_target="tpu_custom_call" | custom-call | tf_op jit(solution)/shard_map/pallas_call | solution.py:233
  38.5 5.2 %shard_map.84 = f32[8,8192]{1,0:T(8,128)} custom-call(f32[8,8448]{1,0:T(8,128)} %shard_map.83.wide, s32[7,8192]{1,0:T(8,128)} %stencil_ref.1, f32[7,8192]{1,0:T(8,128)} %weights_ref.1), custom_call_target="tpu_custom_call" | custom-call | tf_op jit(solution)/shard_map/pallas_call | solution.py:282
